TPU v7x, 256 devices: a whole 4x4x8 slice. The times are simulated.
256 devices in a mesh: subj: 8 (over y, core), vox: 32 (over z, x).
Axes of the slice: x: 4, y: 4, z: 8, core: 2. Of those that a mesh axis runs over, the one named last changes fastest.
Arguments:
- scans: bfloat16 [16, 65536, 1024], P('subj', 'vox'), may hold values from -48 to 48
- start_maps: bfloat16 [16, 64, 65536], P('subj', None, 'vox'), may hold values from -6 to 6
Outputs:
- shared_resp: float32 [64, 1024], P(None, 'vox')
- subject_maps: bfloat16 [16, 64, 65536], P('subj', None, 'vox')
All inputs are finite; a program needn't handle non-finite values.
Results may differ from a plain program's by a relative error of at most 0.011.
Values may be sent and summed in bfloat16 or wider, within the bound.
No kernel may reach another device: no remote copies, remote signals or barrier semaphores. Data moves between devices by JAX's collectives and lax.ppermute only.
A program may use at most 64 MiB of HBM per device.

v0:
```python
import math

import jax
import jax.numpy as jnp
from jax import lax
from jax.sharding import PartitionSpec as P

ITERS = 6


def per_device(scans, start_maps):
    subj_dev = scans.shape[0]
    vox_dev = scans.shape[1]
    frames = scans.shape[2]
    features = start_maps.shape[1]
    voxels = vox_dev * lax.axis_size("vox")
    subjects = subj_dev * lax.axis_size("subj")
    norm_scale = 1.0 / (subjects * math.sqrt(voxels))
    width = frames // lax.axis_size("vox")
    identity = jnp.eye(features, dtype=jnp.float32)
    highest_precision = lax.Precision.HIGHEST

    def update(subject_projections):
        partial_response_value = jnp.einsum(
            "qbf,qfh->bh", subject_projections, scans, preferred_element_type=jnp.float32
        )
        summed = lax.psum(partial_response_value, ("subj", "vox")) * norm_scale
        frame_share = lax.dynamic_slice_in_dim(summed, lax.axis_index("vox") * width, width, 1)
        shared_response_second = summed.astype(jnp.bfloat16)
        projection_target = jnp.einsum(
            "ri,upi->urp", shared_response_second, scans, preferred_element_type=jnp.float32
        )
        squares = lax.psum(jnp.sum(projection_target * projection_target, axis=(1, 2)), "vox")
        newton_iterate = projection_target / jnp.sqrt(squares)[:, None, None]
        for step in range(ITERS):
            subject_gram_matrix = jnp.einsum(
                "rzo,rlo->rzl", newton_iterate, newton_iterate, precision=highest_precision
            )
            gram = lax.psum(subject_gram_matrix.astype(jnp.bfloat16), "vox").astype(jnp.float32)
            polar_matrix = 1.5 * identity[None] - 0.5 * gram
            newton_iterate = jnp.einsum(
                "hzu,huo->hzo", polar_matrix, newton_iterate, precision=highest_precision
            )
        new_maps = (newton_iterate * math.sqrt(voxels)).astype(jnp.bfloat16)
        return (frame_share, new_maps)

    first_share, first_maps = update(start_maps)
    shared_resp, subject_maps = update(first_maps)
    return (shared_resp, subject_maps)


def solution(mesh):
    placed = (P("subj", "vox", None), P("subj", None, "vox"))
    return jax.shard_map(
        per_device,
        mesh=mesh,
        in_specs=placed,
        out_specs=(P(None, "vox"), P("subj", None, "vox")),
        check_vma=False,
    )
```

profile of v0, /device:TPU:8, one launch (start us, length us, event | category | flops | bytes accessed | tf_op | source)
XLA Modules:
  0.0 2366.9 jit_solution(14207118049088847362)
XLA Ops:
  8.2 5.7 convolution_bitcast_fusion.1
  14.0 253.1 %all-reduce.3.cloned.1.call-done = f32[64,1024]{1,0:T(8,128)} async-done(((f32[64,1024]{1,0:T(8,128)}), f32[64,1024]{1,0:T(8,128)}) %all-reduce.3.cloned.1.call-update) | async-done | bytes 262160 | tf_op jit(solution)/shard_map/psum | solution.py:27
  267.1 6.2 multiply_reduce_fusion.1
  273.3 71.8 %psum.113 = f32[2]{0:T(128)S(1)} all-reduce(f32[2]{0:T(128)S(1)} %get-tuple-element.4), channel_id=1, replica_groups=mesh['subj'=8,'vox'=32] {'vox'}, use_global_device_ids=true, to_apply=%region_2.0 | all-reduce | flops 2 | bytes 16 | tf_op jit(solution)/shard_map/psum | solution.py:33
  345.2 1.2 convolution_convert_fusion.11
  346.4 137.7 %psum.114 = bf16[2,64,64]{2,1,0:T(8,128)(2,1)S(1)} all-reduce(bf16[2,64,64]{2,1,0:T(8,128)(2,1)S(1)} %convolution_convert_fusion.11), channel_id=1, replica_groups=mesh['subj'=8,'vox'=32] {'vox'}, use_global_device_ids=true, to_apply=%region_3.0 | all-reduce | flops 8192 | bytes 32768 | tf_op jit(solution)/shard_map/psum | solution.py:39
  485.2 1.1 convolution_convert_fusion.10
  486.3 137.7 %psum.115 = bf16[2,64,64]{2,1,0:T(8,128)(2,1)S(1)} all-reduce(bf16[2,64,64]{2,1,0:T(8,128)(2,1)S(1)} %convolution_convert_fusion.10), channel_id=1, replica_groups=mesh['subj'=8,'vox'=32] {'vox'}, use_global_device_ids=true, to_apply=%region_4.0 | all-reduce | flops 8192 | bytes 32768 | tf_op jit(solution)/shard_map/psum | solution.py:39
  625.0 1.1 convolution_convert_fusion.9
  626.1 137.7 %psum.116 = bf16[2,64,64]{2,1,0:T(8,128)(2,1)S(1)} all-reduce(bf16[2,64,64]{2,1,0:T(8,128)(2,1)S(1)} %convolution_convert_fusion.9), channel_id=1, replica_groups=mesh['subj'=8,'vox'=32] {'vox'}, use_global_device_ids=true, to_apply=%region_5.0 | all-reduce | flops 8192 | bytes 32768 | tf_op jit(solution)/shard_map/psum | solution.py:39
  764.9 1.1 convolution_convert_fusion.8
  766.0 137.9 %psum.117 = bf16[2,64,64]{2,1,0:T(8,128)(2,1)S(1)} all-reduce(bf16[2,64,64]{2,1,0:T(8,128)(2,1)S(1)} %convolution_convert_fusion.8), channel_id=1, replica_groups=mesh['subj'=8,'vox'=32] {'vox'}, use_global_device_ids=true, to_apply=%region_6.0 | all-reduce | flops 8192 | bytes 32768 | tf_op jit(solution)/shard_map/psum | solution.py:39
  906.1 137.7 %psum.118 = bf16[2,64,64]{2,1,0:T(8,128)(2,1)S(1)} all-reduce(bf16[2,64,64]{2,1,0:T(8,128)(2,1)S(1)} %convolution_convert_fusion.7), channel_id=1, replica_groups=mesh['subj'=8,'vox'=32] {'vox'}, use_global_device_ids=true, to_apply=%region_7.0 | all-reduce | flops 8192 | bytes 32768 | tf_op jit(solution)/shard_map/psum | solution.py:39
  1044.8 1.1 convolution_convert_fusion.6
  1045.9 137.7 %psum.119 = bf16[2,64,64]{2,1,0:T(8,128)(2,1)S(1)} all-reduce(bf16[2,64,64]{2,1,0:T(8,128)(2,1)S(1)} %convolution_convert_fusion.6), channel_id=1, replica_groups=mesh['subj'=8,'vox'=32] {'vox'}, use_global_device_ids=true, to_apply=%region_8.0 | all-reduce | flops 8192 | bytes 32768 | tf_op jit(solution)/shard_map/psum | solution.py:39
  1184.7 5.7 convolution_bitcast_fusion
  1190.4 247.4 %all-reduce.5.cloned.1.call-done = f32[64,1024]{1,0:T(8,128)} async-done(((f32[64,1024]{1,0:T(8,128)}), f32[64,1024]{1,0:T(8,128)}) %all-reduce.5.cloned.1.call-update) | async-done | bytes 262160 | tf_op jit(solution)/shard_map/psum | solution.py:27
  1439.5 6.2 multiply_reduce_fusion
  1445.7 71.8 %psum.121 = f32[2]{0:T(128)S(1)} all-reduce(f32[2]{0:T(128)S(1)} %get-tuple-element.6), channel_id=1, replica_groups=mesh['subj'=8,'vox'=32] {'vox'}, use_global_device_ids=true, to_apply=%region_11.0 | all-reduce | flops 2 | bytes 16 | tf_op jit(solution)/shard_map/psum | solution.py:33
  1517.6 1.2 convolution_convert_fusion.5
  1518.8 137.9 %psum.122 = bf16[2,64,64]{2,1,0:T(8,128)(2,1)S(1)} all-reduce(bf16[2,64,64]{2,1,0:T(8,128)(2,1)S(1)} %convolution_convert_fusion.5), channel_id=1, replica_groups=mesh['subj'=8,'vox'=32] {'vox'}, use_global_device_ids=true, to_apply=%region_12.0 | all-reduce | flops 8192 | bytes 32768 | tf_op jit(solution)/shard_map/psum | solution.py:39
  1657.8 1.1 convolution_convert_fusion.4
  1658.9 137.7 %psum.123 = bf16[2,64,64]{2,1,0:T(8,128)(2,1)S(1)} all-reduce(bf16[2,64,64]{2,1,0:T(8,128)(2,1)S(1)} %convolution_convert_fusion.4), channel_id=1, replica_groups=mesh['subj'=8,'vox'=32] {'vox'}, use_global_device_ids=true, to_apply=%region_13.0 | all-reduce | flops 8192 | bytes 32768 | tf_op jit(solution)/shard_map/psum | solution.py:39
  1797.7 1.1 convolution_convert_fusion.3
  1798.8 137.7 %psum.124 = bf16[2,64,64]{2,1,0:T(8,128)(2,1)S(1)} all-reduce(bf16[2,64,64]{2,1,0:T(8,128)(2,1)S(1)} %convolution_convert_fusion.3), channel_id=1, replica_groups=mesh['subj'=8,'vox'=32] {'vox'}, use_global_device_ids=true, to_apply=%region_14.0 | all-reduce | flops 8192 | bytes 32768 | tf_op jit(solution)/shard_map/psum | solution.py:39
  1937.5 1.1 convolution_convert_fusion.2
  1938.6 137.7 %psum.125 = bf16[2,64,64]{2,1,0:T(8,128)(2,1)S(1)} all-reduce(bf16[2,64,64]{2,1,0:T(8,128)(2,1)S(1)} %convolution_convert_fusion.2), channel_id=1, replica_groups=mesh['subj'=8,'vox'=32] {'vox'}, use_global_device_ids=true, to_apply=%region_15.0 | all-reduce | flops 8192 | bytes 32768 | tf_op jit(solution)/shard_map/psum | solution.py:39
  2079.5 137.7 %psum.126 = bf16[2,64,64]{2,1,0:T(8,128)(2,1)S(1)} all-reduce(bf16[2,64,64]{2,1,0:T(8,128)(2,1)S(1)} %convolution_convert_fusion.1), channel_id=1, replica_groups=mesh['subj'=8,'vox'=32] {'vox'}, use_global_device_ids=true, to_apply=%region_16.0 | all-reduce | flops 8192 | bytes 32768 | tf_op jit(solution)/shard_map/psum | solution.py:39
  2217.2 2.2 fusion.18
  2219.4 1.1 convolution_convert_fusion
  2220.5 137.7 %psum.127 = bf16[2,64,64]{2,1,0:T(8,128)(2,1)S(1)} all-reduce(bf16[2,64,64]{2,1,0:T(8,128)(2,1)S(1)} %convolution_convert_fusion), channel_id=1, replica_groups=mesh['subj'=8,'vox'=32] {'vox'}, use_global_device_ids=true, to_apply=%region_17.0 | all-reduce | flops 8192 | bytes 32768 | tf_op jit(solution)/shard_map/psum | solution.py:39
  2358.2 1.8 fusion.1
  (26 shorter events, 16.4 us)
Async XLA Ops:
  7.2 1.0 copy-start
  7.2 259.9 %all-reduce.3.cloned.1.call-start = ((), (), s32[]{:S(2)}) async-start(), calls=%async_computation | async-start | bytes 524288 | tf_op jit(solution)/shard_map/psum | solution.py:27
  13.9 1423.9 %all-reduce.5.cloned.1.call-start = ((), (), s32[]{:S(2)}) async-start(), calls=%async_computation.1 | async-start | bytes 524288 | tf_op jit(solution)/shard_map/psum | solution.py:27
  2077.4 1.0 copy-start.1
Sparse Core Ops, SparseCore 0:
  14.0 252.9 all-reduce.2
  1190.5 247.2 all-reduce.4
where the time goes:
time: 2370 us
  blocking collectives  1800 us (76%)
  waiting for transfers between devices  501 us (21%)
  matrix products  51.6 us (2%)
    psum x12, blocking collectives, update(): lax.psum(subject_gram_matrix.astype(jnp.bfloat16), 'vox')  1650 us
    psum x2, waiting for transfers between devices, update(): summed = lax.psum(partial_response_value, ('subj', 'vox')) * norm_scale  501 us
    psum x2, blocking collectives, update(): lax.psum(jnp.sum(projection_target * projection_target, axis=(1, 2)), 'vox')  144 us
  transfers between devices with their start and end apart: 2, of which 2 were waited for; matrix products, arithmetic and copies ran while one was open for 0% of the time, Pallas kernels for 0%

commit v1 on v0

v1 whole, which is shorter than its diff:
```python
import functools
import math

import jax
import jax.numpy as jnp
from jax import lax
from jax.experimental import pallas as pl
from jax.experimental.pallas import tpu as pltpu
from jax.sharding import PartitionSpec as P

ITERS = 6
HALF = 64
LANES = 128
BF16 = jnp.bfloat16
F32 = jnp.float32
VMEM_LIMIT = 48 * 1024 * 1024
PARAMS = pltpu.CompilerParams(vmem_limit_bytes=VMEM_LIMIT)


def dot(a, b, contract=(1, 0), precision=None):
    return lax.dot_general(
        a,
        b,
        (((contract[0],), (contract[1],)), ((), ())),
        preferred_element_type=F32,
        precision=precision,
    )


def full_dot(a, b):
    return dot(a, b, precision=lax.Precision.HIGHEST)


def grid_rows_cols(n):
    rows = lax.broadcasted_iota(jnp.int32, (n, n), 0)
    cols = lax.broadcasted_iota(jnp.int32, (n, n), 1)
    return rows, cols


def pack_frames(by_frame):
    shares = by_frame.shape[0] // 32
    split = by_frame.reshape(shares, 2, 16, HALF)
    return jnp.concatenate([split[:, 0], split[:, 1]], axis=-1)


def unpack_frames(packed):
    shares = packed.shape[0]
    split = jnp.stack([packed[:, :, :HALF], packed[:, :, HALF:]], axis=1)
    return split.reshape(shares * 32, HALF)


def pack_grams(first, second):
    rows, cols = grid_rows_cols(HALF)
    joined = jnp.where(rows <= cols, first, second)
    wide = jnp.concatenate([joined[:32], joined[32:]], axis=1)
    diagonal = jnp.sum(jnp.where(rows == cols, second, 0.0), axis=0, keepdims=True)
    diagonal = jnp.concatenate([diagonal, diagonal], axis=1)
    return jnp.concatenate([wide, jnp.broadcast_to(diagonal, (16, LANES))], axis=0)


def unpack_grams(packed):
    rows, cols = grid_rows_cols(HALF)
    joined = jnp.concatenate([packed[:32, :HALF], packed[:32, HALF:]], axis=0)
    flipped = joined.T
    diagonal = packed[32:33, :HALF]
    first = jnp.where(rows <= cols, joined, flipped)
    second = jnp.where(rows > cols, joined, jnp.where(rows == cols, diagonal, flipped))
    return first, second


def polar_factors(first, second):
    rows, cols = grid_rows_cols(HALF)
    on_diagonal = rows == cols
    zero = jnp.zeros((HALF, HALF), F32)

    def trace(gram):
        return jnp.sum(jnp.where(on_diagonal, gram, 0.0), keepdims=True)

    squares = trace(first), trace(second)
    gram = jnp.concatenate(
        [
            jnp.concatenate([first / squares[0], zero], axis=1),
            jnp.concatenate([zero, second / squares[1]], axis=1),
        ],
        axis=0,
    )
    big_rows, big_cols = grid_rows_cols(LANES)
    identity = jnp.where(big_rows == big_cols, 1.0, 0.0)
    factor = None
    for step in range(ITERS):
        polar = 1.5 * identity - 0.5 * gram
        factor = polar if factor is None else full_dot(polar, factor)
        if step < ITERS - 1:
            gram = full_dot(full_dot(polar, gram), polar)
    scale = jnp.where(
        big_rows[:, :1] < HALF, lax.rsqrt(squares[0]), lax.rsqrt(squares[1])
    )
    return factor * scale


def start_kernel(maps_ref, scans_ref, out_ref, total):
    first = (pl.program_id(0) == 0) & (pl.program_id(1) == 0)
    last = (pl.program_id(0) == pl.num_programs(0) - 1) & (
        pl.program_id(1) == pl.num_programs(1) - 1
    )

    @pl.when(first)
    def _():
        total[...] = jnp.zeros_like(total)

    total[...] += dot(maps_ref[0], scans_ref[0])

    @pl.when(last)
    def _():
        out_ref[...] = pack_frames(total[...].T).astype(BF16)


def add_kernel(scale, parts_ref, out_ref):
    summed = jnp.sum(parts_ref[...].astype(F32), axis=0) * scale
    out_ref[...] = jnp.broadcast_to(summed[None], out_ref.shape)


def spread_kernel(parts_ref, out_ref):
    summed = jnp.sum(parts_ref[...], axis=0)
    out_ref[...] = jnp.broadcast_to(summed.astype(BF16)[None], out_ref.shape)


def spread_last_kernel(parts_ref, out_ref, resp_ref):
    summed = jnp.sum(parts_ref[...], axis=0)
    out_ref[...] = jnp.broadcast_to(summed.astype(BF16)[None], out_ref.shape)
    resp_ref[...] = unpack_frames(summed[None]).T


def load_shared(packed_ref, shared):
    shared[...] = unpack_frames(packed_ref[...]).T


def middle_kernel(packed_ref, scans_ref, out_ref, shared, gram, onward):
    subject, tile = pl.program_id(0), pl.program_id(1)
    last = tile == pl.num_programs(1) - 1

    @pl.when((subject == 0) & (tile == 0))
    def _():
        load_shared(packed_ref, shared)

    @pl.when(tile == 0)
    def _():
        gram[subject] = jnp.zeros_like(gram[subject])
        onward[subject] = jnp.zeros_like(onward[subject])

    scans = scans_ref[0]
    target = dot(shared[...], scans, (1, 1)).astype(BF16)
    gram[subject] += dot(target, target, (1, 1))
    onward[subject] += dot(target, scans)

    @pl.when(last & (subject == pl.num_programs(0) - 1))
    def _():
        by_frame = jnp.concatenate([onward[0].T, onward[1].T], axis=1)
        shares = out_ref.shape[0]
        out_ref[:, :32, :] = by_frame.reshape(shares, 32, LANES).astype(BF16)
        grams = pack_grams(gram[0], gram[1]).astype(BF16)
        out_ref[:, 32:, :] = jnp.broadcast_to(grams[None], (shares,) + grams.shape)


def polar_share_kernel(scale, parts_ref, out_ref):
    summed = jnp.sum(parts_ref[...].astype(F32), axis=0)
    factor = polar_factors(*unpack_grams(summed[32:]))
    stacked = jnp.concatenate([factor[:HALF, :HALF], factor[HALF:, HALF:]], axis=0)
    share = full_dot(summed[:32], stacked) * scale
    packed = pack_frames(share)
    out_ref[...] = jnp.broadcast_to(packed, out_ref.shape)


def target_kernel(packed_ref, scans_ref, target_ref, out_ref, shared, gram):
    subject, tile = pl.program_id(0), pl.program_id(1)
    last = tile == pl.num_programs(1) - 1

    @pl.when((subject == 0) & (tile == 0))
    def _():
        load_shared(packed_ref, shared)

    @pl.when(tile == 0)
    def _():
        gram[subject] = jnp.zeros_like(gram[subject])

    target = dot(shared[...], scans_ref[0], (1, 1)).astype(BF16)
    target_ref[0] = target
    gram[subject] += dot(target, target, (1, 1))

    @pl.when(last & (subject == pl.num_programs(0) - 1))
    def _():
        grams = pack_grams(gram[0], gram[1]).astype(BF16)
        out_ref[...] = jnp.broadcast_to(grams[None], out_ref.shape)


def maps_kernel(scale, parts_ref, target_ref, out_ref):
    summed = jnp.sum(parts_ref[...].astype(F32), axis=0)
    factor = polar_factors(*unpack_grams(summed)) * scale
    high = factor.astype(BF16)
    low = (factor - high.astype(F32)).astype(BF16)
    for subject in range(2):
        own = slice(subject * HALF, (subject + 1) * HALF)
        target = target_ref[subject]
        maps = dot(high[own, own], target) + dot(low[own, own], target)
        out_ref[subject] = maps.astype(BF16)


def whole(shape):
    return pl.BlockSpec(shape, lambda *_: (0,) * len(shape))


def small(body, out_shape, *args):
    return pl.pallas_call(body, out_shape=out_shape, compiler_params=PARAMS)(*args)


def shape_of(shape, dtype):
    return jax.ShapeDtypeStruct(shape, dtype)


def per_device(scans, start_maps):
    subj_dev, vox_dev, frames = scans.shape
    features = start_maps.shape[1]
    vox_ways, subj_ways = lax.axis_size("vox"), lax.axis_size("subj")
    voxels = vox_dev * vox_ways
    subjects = subj_dev * subj_ways
    norm_scale = 1.0 / (subjects * math.sqrt(voxels))
    tile = 1024
    grid = (subj_dev, vox_dev // tile)
    scans_spec = pl.BlockSpec((1, tile, frames), lambda i, t: (i, t, 0))
    share = (16, LANES)

    def across_vox(x):
        return lax.all_to_all(x, "vox", 0, 0)

    def across_subj(x):
        return lax.all_to_all(x, "subj", 0, 0)

    partial = pl.pallas_call(
        start_kernel,
        out_shape=shape_of((vox_ways,) + share, BF16),
        grid=grid,
        in_specs=[
            pl.BlockSpec((1, features, tile), lambda i, t: (i, 0, t)),
            scans_spec,
        ],
        out_specs=whole((vox_ways,) + share),
        scratch_shapes=[pltpu.VMEM((features, frames), F32)],
        compiler_params=PARAMS,
    )(start_maps, scans)
    parts = across_vox(partial)
    parts = across_subj(
        small(
            functools.partial(add_kernel, norm_scale),
            shape_of((subj_ways,) + share, F32),
            parts,
        )
    )
    shared = across_vox(
        small(spread_kernel, shape_of((vox_ways,) + share, BF16), parts)
    )

    rows = 32 + 48
    partial = pl.pallas_call(
        middle_kernel,
        out_shape=shape_of((vox_ways, rows, LANES), BF16),
        grid=grid,
        in_specs=[whole((vox_ways,) + share), scans_spec],
        out_specs=whole((vox_ways, rows, LANES)),
        scratch_shapes=[
            pltpu.VMEM((features, frames), BF16),
            pltpu.VMEM((subj_dev, features, features), F32),
            pltpu.VMEM((subj_dev, features, frames), F32),
        ],
        compiler_params=PARAMS,
    )(shared, scans)
    parts = across_vox(partial)
    parts = across_subj(
        small(
            functools.partial(polar_share_kernel, 1.0 / subjects),
            shape_of((subj_ways,) + share, F32),
            parts,
        )
    )
    shared, shared_resp = small(
        spread_last_kernel,
        [shape_of((vox_ways,) + share, BF16), shape_of((features, 32), F32)],
        parts,
    )
    shared = across_vox(shared)

    target, partial = pl.pallas_call(
        target_kernel,
        out_shape=[
            shape_of((subj_dev, features, vox_dev), BF16),
            shape_of((vox_ways, 48, LANES), BF16),
        ],
        grid=grid,
        in_specs=[whole((vox_ways,) + share), scans_spec],
        out_specs=[
            pl.BlockSpec((1, features, tile), lambda i, t: (i, 0, t)),
            whole((vox_ways, 48, LANES)),
        ],
        scratch_shapes=[
            pltpu.VMEM((features, frames), BF16),
            pltpu.VMEM((subj_dev, features, features), F32),
        ],
        compiler_params=PARAMS,
    )(shared, scans)
    parts = across_vox(partial)
    subject_maps = small(
        functools.partial(maps_kernel, math.sqrt(voxels)),
        shape_of((subj_dev, features, vox_dev), BF16),
        parts,
        target,
    )
    return (shared_resp, subject_maps)


def solution(mesh):
    placed = (P("subj", "vox", None), P("subj", None, "vox"))
    return jax.shard_map(
        per_device,
        mesh=mesh,
        in_specs=placed,
        out_specs=(P(None, "vox"), P("subj", None, "vox")),
        check_vma=False,
    )
```

time: 2370 us -> 138 us (0.06)
  blocking collectives: 1800 us -> 89.9 us
  waiting for transfers between devices: 501 us -> 13.8 us
  matrix products: 51.6 us -> 0 us
  Pallas kernels: 0 us -> 27.4 us
    psum x14 -> x0, blocking collectives: 1800 us -> none  [the longest x12 1650 us: update(): lax.psum(subject_gram_matrix.astype(jnp.bfloat16), 'vox')]
    psum x2 -> x0, waiting for transfers between devices: 501 us -> none  [update(): summed = lax.psum(partial_response_value, ('subj', 'vox')) * norm_scale]
    all_to_all x0 -> x6, blocking collectives: none -> 89.9 us  [the longest x4 73 us: across_vox(): return lax.all_to_all(x, 'vox', 0, 0)]
    dot_general x28 -> x0, matrix products: 51.6 us -> none  [the longest x12 14.4 us: update(): jnp.einsum('hzu,huo->hzo', polar_matrix, newton_iterate, precision=highes...]
    pallas_call x0 -> x8, Pallas kernels: none -> 27.4 us  [the longest x1 7.64 us: per_device(): pl.pallas_call(middle_kernel, out_shape=shape_of((vox_ways, rows, LANES),...]
  transfers between devices with their start and end apart: 2 -> 1, of which waited for: 2 -> 1; matrix products, arithmetic and copies ran while one was open for 0% -> 0% of each run, Pallas kernels for 0% -> 0%
where the time goes in v1:
time: 138 us; the launch traced here: 137 us
  blocking collectives  89.9 us (65%)
  Pallas kernels  27.4 us (20%)
  waiting for transfers between devices  13.8 us (10%)
  starting transfers between devices  3.88 us (3%)
  local copies, waits for them, and re-layouts  1.72 us (1%)
    all_to_all x4, blocking collectives, across_vox(): return lax.all_to_all(x, 'vox', 0, 0)  73 us
    all_to_all x2, blocking collectives, across_subj(): return lax.all_to_all(x, 'subj', 0, 0)  16.9 us
    all_to_all x1, waiting for transfers between devices, across_vox(): return lax.all_to_all(x, 'vox', 0, 0)  13.8 us
    pallas_call x1, Pallas kernels, per_device(): pl.pallas_call(middle_kernel, out_shape=shape_of((vox_ways, rows, LANES),...  7.64 us
    pallas_call x5, Pallas kernels, small(): pl.pallas_call(body, out_shape=out_shape, compiler_params=PARAMS)(*args)  7.34 us
    pallas_call x1, Pallas kernels, per_device(): pl.pallas_call(target_kernel, out_shape=[shape_of((subj_dev, features, vo...  7.19 us
    pallas_call x1, Pallas kernels, per_device(): pl.pallas_call(start_kernel, out_shape=shape_of((vox_ways,) + share, BF16...  5.21 us
    all_to_all x1, starting transfers between devices, across_vox(): return lax.all_to_all(x, 'vox', 0, 0)  3.88 us
  transfers between devices with their start and end apart: 1, of which 1 were waited for; matrix products, arithmetic and copies ran while one was open for 0% of the time, Pallas kernels for 0%

profile of v1, /device:TPU:8, one launch (start us, length us, event | category | flops | bytes accessed | tf_op | source)
XLA Modules:
  0.0 137.3 jit_solution(15355810220860892868)
XLA Ops:
  0.6 0.0 copy-start
  0.6 1.0 copy-done
  1.7 5.2 %shard_map.41 = bf16[32,16,128]{2,1,0:T(8,128)(2,1)S(1)} custom-call(bf16[2,64,2048]{2,1,0:T(8,128)(2,1)S(1)} %copy-done, bf16[2,2048,1024]{2,1,0:T(8,128)(2,1)} %scans_ref.5), custom_call_target="tpu_custom_call" | custom-call | tf_op jit(solution)/shard_map/pallas_call | solution.py:238
  6.9 21.6 %all_to_all.35.parts_ref = bf16[32,16,128]{2,1,0:T(8,128)(2,1)S(1)} all-to-all(bf16[32,16,128]{2,1,0:T(8,128)(2,1)S(1)} %shard_map.41), channel_id=1, replica_groups=mesh['subj'=8,'vox'=32] {'vox'}, dimensions={0} | all-to-all | bytes 262144 | tf_op jit(solution)/shard_map/all_to_all | solution.py:233
  28.5 8.9 %all_to_all.36.parts_ref = f32[8,16,128]{2,1,0:T(8,128)S(1)} all-to-all(f32[8,16,128]{2,1,0:T(8,128)S(1)} %shard_map.42), channel_id=1, replica_groups=mesh['subj'=8,'vox'=32] {'subj'}, dimensions={0} | all-to-all | bytes 131072 | tf_op jit(solution)/shard_map/all_to_all | solution.py:236
  37.4 13.9 %all_to_all.37.packed_ref = bf16[32,16,128]{2,1,0:T(8,128)(2,1)S(1)} all-to-all(bf16[32,16,128]{2,1,0:T(8,128)(2,1)S(1)} %shard_map.43), channel_id=1, replica_groups=mesh['subj'=8,'vox'=32] {'vox'}, dimensions={0} | all-to-all | bytes 262144 | tf_op jit(solution)/shard_map/all_to_all | solution.py:233
  51.3 7.6 %shard_map.44 = bf16[32,80,128]{2,1,0:T(8,128)(2,1)S(1)} custom-call(bf16[32,16,128]{2,1,0:T(8,128)(2,1)S(1)} %all_to_all.37.packed_ref, bf16[2,2048,1024]{2,1,0:T(8,128)(2,1)} %scans_ref.5), custom_call_target="tpu_custom_call" | custom-call | tf_op jit(solution)/shard_map/pallas_call | solution.py:263
  58.9 22.5 %all_to_all.38.parts_ref = bf16[32,80,128]{2,1,0:T(8,128)(2,1)S(1)} all-to-all(bf16[32,80,128]{2,1,0:T(8,128)(2,1)S(1)} %shard_map.44), channel_id=1, replica_groups=mesh['subj'=8,'vox'=32] {'vox'}, dimensions={0} | all-to-all | bytes 1310720 | tf_op jit(solution)/shard_map/all_to_all | solution.py:233
  81.4 3.1 %shard_map.45 = f32[8,16,128]{2,1,0:T(8,128)S(1)} custom-call(bf16[32,80,128]{2,1,0:T(8,128)(2,1)S(1)} %all_to_all.38.parts_ref), custom_call_target="tpu_custom_call" | custom-call | tf_op jit(solution)/shard_map/pallas_call | solution.py:213
  84.6 8.0 %all_to_all.39.parts_ref = f32[8,16,128]{2,1,0:T(8,128)S(1)} all-to-all(f32[8,16,128]{2,1,0:T(8,128)S(1)} %shard_map.45), channel_id=1, replica_groups=mesh['subj'=8,'vox'=32] {'subj'}, dimensions={0} | all-to-all | bytes 131072 | tf_op jit(solution)/shard_map/all_to_all | solution.py:236
  92.6 0.2 shard_map.46
  92.7 15.0 %all_to_all.40.packed_ref = bf16[32,16,128]{2,1,0:T(8,128)(2,1)S(1)} all-to-all(bf16[32,16,128]{2,1,0:T(8,128)(2,1)S(1)} %get-tuple-element.7), channel_id=1, replica_groups=mesh['subj'=8,'vox'=32] {'vox'}, dimensions={0} | all-to-all | bytes 262144 | tf_op jit(solution)/shard_map/all_to_all | solution.py:233
  107.7 7.2 %shard_map.47 = (bf16[2,64,2048]{2,1,0:T(8,128)(2,1)S(1)}, bf16[32,48,128]{2,1,0:T(8,128)(2,1)}) custom-call(bf16[32,16,128]{2,1,0:T(8,128)(2,1)S(1)} %all_to_all.40.packed_ref, bf16[2,2048,1024]{2,1,0:T(8,128)(2,1)} %scans_ref.5), custom_call_target="tpu_custom_call" | custom-call | tf_op jit(solution)/shard_map/pallas_call | solution.py:291
  114.9 3.9 %all-to-all-start.6 = ((bf16[32,48,128]{2,1,0:T(8,128)(2,1)}), bf16[32,48,128]{2,1,0:T(8,128)(2,1)S(1)}, u32[]{:S(2)}, u32[]{:S(2)}) async-start(bf16[32,48,128]{2,1,0:T(8,128)(2,1)} %get-tuple-element.8), calls=%async_computation.6 | async-start | bytes 786432 | tf_op jit(solution)/shard_map/all_to_all | solution.py:233
  118.8 0.7 copy.4
  119.5 13.8 %all-to-all-done.6.parts_ref = bf16[32,48,128]{2,1,0:T(8,128)(2,1)S(1)} async-done(((bf16[32,48,128]{2,1,0:T(8,128)(2,1)}), bf16[32,48,128]{2,1,0:T(8,128)(2,1)S(1)}, u32[]{:S(2)}, u32[]{:S(2)}) %all-to-all-start.6) | async-done | bytes 393248 | tf_op jit(solution)/shard_map/all_to_all | solution.py:233
  133.3 4.0 %shard_map.48 = bf16[2,64,2048]{2,1,0:T(8,128)(2,1)} custom-call(bf16[32,48,128]{2,1,0:T(8,128)(2,1)S(1)} %all-to-all-done.6.parts_ref, bf16[2,64,2048]{2,1,0:T(8,128)(2,1)S(1)} %get-tuple-element.9.target_ref), custom_call_target="tpu_custom_call" | custom-call | tf_op jit(solution)/shard_map/pallas_call | solution.py:213
  (2 shorter events, 0.1 us)
Async XLA Ops:
  0.6 1.0 copy-start
  114.9 18.3 %all-to-all-start.6 = ((bf16[32,48,128]{2,1,0:T(8,128)(2,1)}), bf16[32,48,128]{2,1,0:T(8,128)(2,1)S(1)}, u32[]{:S(2)}, u32[]{:S(2)}) async-start(bf16[32,48,128]{2,1,0:T(8,128)(2,1)} %get-tuple-element.8), calls=%async_computation.6 | async-start | bytes 786432 | tf_op jit(solution)/shard_map/all_to_all | solution.py:233

commit v2 on v1

v2 whole, which is shorter than its diff:
```python
import functools
import math

import jax
import jax.numpy as jnp
from jax import lax
from jax.experimental import pallas as pl
from jax.experimental.pallas import tpu as pltpu
from jax.sharding import PartitionSpec as P

ITERS = 6
HALF = 64
LANES = 128
X_WAYS = 4
BF16 = jnp.bfloat16
F32 = jnp.float32
MIB = 1024 * 1024
PARAMS = pltpu.CompilerParams(vmem_limit_bytes=24 * MIB)
START_PARAMS = pltpu.CompilerParams(vmem_limit_bytes=42 * MIB)


def dot(a, b, contract=(1, 0), precision=None):
    return lax.dot_general(
        a,
        b,
        (((contract[0],), (contract[1],)), ((), ())),
        preferred_element_type=F32,
        precision=precision,
    )


def halves(x):
    high = x.astype(BF16)
    return high, (x - high.astype(F32)).astype(BF16)


def split_dot(a, b):
    a_high, a_low = halves(a)
    b_high, b_low = halves(b)
    left = jnp.concatenate([a_high, a_low], axis=1)
    right = jnp.concatenate(
        [
            jnp.concatenate([b_high, b_low], axis=1),
            jnp.concatenate([b_high, b_low], axis=1),
        ],
        axis=0,
    )
    both = dot(left, right)
    width = b.shape[1]
    return both[:, :width] + both[:, width:]


def grid_rows_cols(n):
    rows = lax.broadcasted_iota(jnp.int32, (n, n), 0)
    cols = lax.broadcasted_iota(jnp.int32, (n, n), 1)
    return rows, cols


def pack_frames(by_frame):
    shares = by_frame.shape[0] // 32
    split = by_frame.reshape(shares, 2, 16, HALF)
    return jnp.concatenate([split[:, 0], split[:, 1]], axis=-1)


def unpack_frames(packed):
    shares = packed.shape[0]
    split = jnp.stack([packed[:, :, :HALF], packed[:, :, HALF:]], axis=1)
    return split.reshape(shares * 32, HALF)


def pack_grams(first, second):
    rows, cols = grid_rows_cols(HALF)
    joined = jnp.where(rows <= cols, first, second)
    wide = jnp.concatenate([joined[:32], joined[32:]], axis=1)
    diagonal = jnp.sum(jnp.where(rows == cols, second, 0.0), axis=0, keepdims=True)
    diagonal = jnp.concatenate([diagonal, diagonal], axis=1)
    return jnp.concatenate([wide, jnp.broadcast_to(diagonal, (8, LANES))], axis=0)


def unpack_grams(packed):
    rows, cols = grid_rows_cols(HALF)
    joined = jnp.concatenate([packed[:32, :HALF], packed[:32, HALF:]], axis=0)
    flipped = joined.T
    diagonal = packed[32:33, :HALF]
    first = jnp.where(rows <= cols, joined, flipped)
    second = jnp.where(rows > cols, joined, jnp.where(rows == cols, diagonal, flipped))
    return first, second


def polar_factors(first, second):
    rows, cols = grid_rows_cols(HALF)
    on_diagonal = rows == cols
    zero = jnp.zeros((HALF, HALF), F32)

    def trace(gram):
        return jnp.sum(jnp.where(on_diagonal, gram, 0.0), keepdims=True)

    squares = trace(first), trace(second)
    gram = jnp.concatenate(
        [
            jnp.concatenate([first / squares[0], zero], axis=1),
            jnp.concatenate([zero, second / squares[1]], axis=1),
        ],
        axis=0,
    )
    big_rows, big_cols = grid_rows_cols(LANES)
    identity = jnp.where(big_rows == big_cols, 1.0, 0.0)
    factor = None
    for step in range(ITERS):
        polar = 1.5 * identity - 0.5 * gram
        factor = polar if factor is None else split_dot(polar, factor)
        if step < ITERS - 1:
            gram = split_dot(split_dot(polar, gram), polar)
    scale = jnp.where(
        big_rows[:, :1] < HALF, lax.rsqrt(squares[0]), lax.rsqrt(squares[1])
    )
    return factor * scale


def start_kernel(tile, maps_ref, scans_ref, out_ref, held, maps, maps_sem, sems):
    subjects, voxels, frames = held.shape
    maps_copy = pltpu.make_async_copy(maps_ref, maps, maps_sem)
    maps_copy.start()
    copies = []
    for subject in range(subjects):
        for begin in range(0, voxels, tile):
            part = (subject, slice(begin, begin + tile))
            copy = pltpu.make_async_copy(
                scans_ref.at[part], held.at[part], sems.at[len(copies)]
            )
            copy.start()
            copies.append((copy, part))
    maps_copy.wait()
    total = jnp.zeros((maps.shape[1], frames), F32)
    for copy, part in copies:
        copy.wait()
        total += dot(maps[part[0], :, part[1]], held[part])
    out_ref[...] = pack_frames(total.T).astype(BF16)


def add_kernel(scale, parts_ref, out_ref):
    summed = jnp.sum(parts_ref[...].astype(F32), axis=0) * scale
    out_ref[...] = jnp.broadcast_to(summed[None], out_ref.shape)


def spread_kernel(parts_ref, out_ref):
    summed = jnp.sum(parts_ref[...], axis=0)
    out_ref[...] = jnp.broadcast_to(summed.astype(BF16)[None], out_ref.shape)


def spread_last_kernel(parts_ref, out_ref, resp_ref):
    summed = jnp.sum(parts_ref[...], axis=0)
    out_ref[...] = jnp.broadcast_to(summed.astype(BF16)[None], out_ref.shape)
    resp_ref[...] = unpack_frames(summed[None]).T


def middle_kernel(packed_ref, scans_ref, out_ref):
    shared = unpack_frames(packed_ref[...]).T
    grams, onward = [], []
    for subject in range(2):
        scans = scans_ref[subject]
        target = dot(shared, scans, (1, 1)).astype(BF16)
        grams.append(dot(target, target, (1, 1)))
        onward.append(dot(target, scans).T)
    shares = out_ref.shape[0]
    by_frame = jnp.concatenate(onward, axis=1).reshape(shares, 32, LANES)
    packed = pack_grams(*grams)
    packed = jnp.broadcast_to(packed[None], (shares,) + packed.shape)
    out_ref[...] = jnp.concatenate([by_frame, packed], axis=1).astype(BF16)


def polar_share_kernel(scale, parts_ref, out_ref):
    summed = jnp.sum(parts_ref[...].astype(F32), axis=0)
    factor = polar_factors(*unpack_grams(summed[32:]))
    stacked = jnp.concatenate([factor[:HALF, :HALF], factor[HALF:, HALF:]], axis=0)
    high, low = halves(summed[:32])
    stack_high, stack_low = halves(stacked)
    share = dot(high, stack_high) + dot(low, stack_high) + dot(high, stack_low)
    share *= scale
    packed = pack_frames(share)
    out_ref[...] = jnp.broadcast_to(packed, out_ref.shape)


def target_kernel(packed_ref, scans_ref, target_ref, out_ref):
    shared = unpack_frames(packed_ref[...]).T
    grams = []
    for subject in range(2):
        target = dot(shared, scans_ref[subject], (1, 1)).astype(BF16)
        target_ref[subject] = target
        grams.append(dot(target, target, (1, 1)))
    packed = pack_grams(*grams).astype(BF16)
    out_ref[...] = jnp.broadcast_to(packed[None], out_ref.shape)


def maps_kernel(scale, parts_ref, target_ref, out_ref):
    summed = jnp.sum(parts_ref[...].astype(F32), axis=0)
    factor = polar_factors(*unpack_grams(summed)) * scale
    high = factor.astype(BF16)
    low = (factor - high.astype(F32)).astype(BF16)
    for subject in range(2):
        own = slice(subject * HALF, (subject + 1) * HALF)
        target = target_ref[subject]
        maps = dot(high[own, own], target) + dot(low[own, own], target)
        out_ref[subject] = maps.astype(BF16)


VMEM = pl.BlockSpec(memory_space=pltpu.VMEM)
HBM = pl.BlockSpec(memory_space=pltpu.HBM)


def shape_of(shape, dtype):
    return jax.ShapeDtypeStruct(shape, dtype)


def small(body, out_shape, *args):
    return pl.pallas_call(
        body,
        out_shape=out_shape,
        in_specs=[VMEM] * len(args),
        out_specs=jax.tree.map(lambda _: VMEM, out_shape),
        compiler_params=PARAMS,
    )(*args)


def start(maps, scans, shares, tile):
    subj_dev, features, vox_dev = maps.shape
    return pl.pallas_call(
        functools.partial(start_kernel, tile),
        out_shape=[
            shape_of((shares, 16, LANES), BF16),
            shape_of(scans.shape, scans.dtype),
        ],
        in_specs=[HBM, HBM],
        out_specs=[VMEM, VMEM],
        scratch_shapes=[
            pltpu.VMEM(maps.shape, maps.dtype),
            pltpu.SemaphoreType.DMA,
            pltpu.SemaphoreType.DMA((subj_dev * (vox_dev // tile),)),
        ],
        compiler_params=START_PARAMS,
    )(maps, scans)


def per_device(scans, start_maps):
    subj_dev, vox_dev, frames = scans.shape
    features = start_maps.shape[1]
    vox_ways, subj_ways = lax.axis_size("vox"), lax.axis_size("subj")
    voxels = vox_dev * vox_ways
    subjects = subj_dev * subj_ways
    norm_scale = 1.0 / (subjects * math.sqrt(voxels))
    share = (16, LANES)
    z_ways = vox_ways // X_WAYS
    same_x = [[z * X_WAYS + x for z in range(z_ways)] for x in range(X_WAYS)]
    same_z = [
        [s * vox_ways + z * X_WAYS + x for s in range(subj_ways) for x in range(X_WAYS)]
        for z in range(z_ways)
    ]

    def across_vox(x):
        return lax.all_to_all(x, "vox", 0, 0)

    def across_subj(x):
        return lax.all_to_all(x, "subj", 0, 0)

    def across_z(x):
        return lax.all_to_all(x, "vox", 0, 0, axis_index_groups=same_x)

    def across_subj_x(x):
        return lax.all_to_all(x, ("subj", "vox"), 0, 0, axis_index_groups=same_z)

    shares = subj_ways * X_WAYS
    partial, scans = start(start_maps, scans, shares, 512)
    parts = across_subj_x(partial)
    summed = functools.partial(add_kernel, norm_scale)
    parts = across_z(small(summed, shape_of((z_ways,) + share, F32), parts))
    shared = small(spread_kernel, shape_of((shares,) + share, BF16), parts)
    shared = across_subj_x(shared)

    partial = small(
        middle_kernel, shape_of((vox_ways, 72, LANES), BF16), shared, scans
    )
    parts = across_vox(partial)
    share_sum = functools.partial(polar_share_kernel, 1.0 / subjects)
    parts = across_subj(small(share_sum, shape_of((subj_ways,) + share, F32), parts))
    shared, shared_resp = small(
        spread_last_kernel,
        [shape_of((vox_ways,) + share, BF16), shape_of((features, 32), F32)],
        parts,
    )
    shared = across_vox(shared)

    target, partial = small(
        target_kernel,
        [
            shape_of((subj_dev, features, vox_dev), BF16),
            shape_of((vox_ways, 40, LANES), BF16),
        ],
        shared,
        scans,
    )
    parts = across_vox(partial)
    subject_maps = small(
        functools.partial(maps_kernel, math.sqrt(voxels)),
        shape_of((subj_dev, features, vox_dev), BF16),
        parts,
        target,
    )
    return (shared_resp, subject_maps)


def solution(mesh):
    placed = (P("subj", "vox", None), P("subj", None, "vox"))
    return jax.shard_map(
        per_device,
        mesh=mesh,
        in_specs=placed,
        out_specs=(P(None, "vox"), P("subj", None, "vox")),
        check_vma=False,
    )
```

time: 138 us -> 125 us (0.906)
  Pallas kernels: 27.4 us -> 17.9 us
  blocking collectives: 89.9 us -> 87.6 us
    all_to_all x0 -> x3, blocking collectives: none -> 41.9 us  [the longest x2 25.3 us: across_subj_x(): return lax.all_to_all(x, ('subj', 'vox'), 0, 0, axis_index_groups=same_z)]
    all_to_all x4 -> x2, blocking collectives: 73 us -> 37.8 us  [across_vox(): return lax.all_to_all(x, 'vox', 0, 0)]
    pallas_call x8, Pallas kernels: 27.4 us -> 17.9 us  [the longest x7 13.8 us: small(): pl.pallas_call(body, out_shape=out_shape, in_specs=[VMEM] * len(args), ou...]
    all_to_all x2 -> x1, blocking collectives: 16.9 us -> 7.95 us  [across_subj(): return lax.all_to_all(x, 'subj', 0, 0)]
  transfers between devices with their start and end apart: 1 -> 1, of which waited for: 1 -> 1; matrix products, arithmetic and copies ran while one was open for 0% -> 1% of each run, Pallas kernels for 0% -> 0%
where the time goes in v2:
time: 125 us; the launch traced here: 124 us
  blocking collectives  87.6 us (70%)
  Pallas kernels  17.9 us (14%)
  waiting for transfers between devices  12.5 us (10%)
  starting transfers between devices  3.88 us (3%)
  local copies, waits for them, and re-layouts  1.72 us (1%)
    all_to_all x2, blocking collectives, across_vox(): return lax.all_to_all(x, 'vox', 0, 0)  37.8 us
    all_to_all x2, blocking collectives, across_subj_x(): return lax.all_to_all(x, ('subj', 'vox'), 0, 0, axis_index_groups=same_z)  25.3 us
    all_to_all x1, blocking collectives, across_z(): return lax.all_to_all(x, 'vox', 0, 0, axis_index_groups=same_x)  16.6 us
    pallas_call x7, Pallas kernels, small(): pl.pallas_call(body, out_shape=out_shape, in_specs=[VMEM] * len(args), ou...  13.8 us
    all_to_all x1, waiting for transfers between devices, across_vox(): return lax.all_to_all(x, 'vox', 0, 0)  12.5 us
    all_to_all x1, blocking collectives, across_subj(): return lax.all_to_all(x, 'subj', 0, 0)  7.95 us
    pallas_call x1, Pallas kernels, start(): pl.pallas_call(functools.partial(start_kernel, tile), out_shape=[shape_of...  4.03 us
    all_to_all x1, starting transfers between devices, across_vox(): return lax.all_to_all(x, 'vox', 0, 0)  3.88 us
  transfers between devices with their start and end apart: 1, of which 1 were waited for; matrix products, arithmetic and copies ran while one was open for 1% of the time, Pallas kernels for 0%

profile of v2, /device:TPU:8, one launch (start us, length us, event | category | flops | bytes accessed | tf_op | source)
XLA Modules:
  0.0 124.2 jit_solution(6403376362529863746)
XLA Ops:
  0.6 0.0 copy-start
  0.6 1.0 copy-done
  1.7 4.0 %shard_map.41 = (bf16[32,16,128]{2,1,0:T(8,128)(2,1)S(1)}, bf16[2,2048,1024]{2,1,0:T(8,128)(2,1)S(1)}) custom-call(bf16[2,64,2048]{2,1,0:T(8,128)(2,1)S(1)} %copy-done, bf16[2,2048,1024]{2,1,0:T(8,128)(2,1)} %scans_ref.1), custom_call_target="tpu_custom_call" | custom-call | tf_op jit(solution)/shard_map/pallas_call | solution.py:227
  5.7 13.8 %all_to_all.35.parts_ref = bf16[32,16,128]{2,1,0:T(8,128)(2,1)S(1)} all-to-all(bf16[32,16,128]{2,1,0:T(8,128)(2,1)S(1)} %get-tuple-element.8), channel_id=1, replica_groups={{0,1,2,3,32,33,34,35,64,65,66,67,96,97,98,99,128,129,130,131,160,161,16..., dimensions={0} | all-to-all | bytes 262144 | tf_op jit(solution)/shard_map/all_to_all | solution.py:269
  19.6 16.6 %all_to_all.36.parts_ref = f32[8,16,128]{2,1,0:T(8,128)S(1)} all-to-all(f32[8,16,128]{2,1,0:T(8,128)S(1)} %shard_map.42), channel_id=1, replica_groups={{0,4,8,12,16,20,24,28},{1,5,9,13,17,21,25,29},{2,6,10,14,18,22,26,30},{..., dimensions={0} | all-to-all | bytes 131072 | tf_op jit(solution)/shard_map/all_to_all | solution.py:266
  36.3 11.5 %all_to_all.37.packed_ref = bf16[32,16,128]{2,1,0:T(8,128)(2,1)S(1)} all-to-all(bf16[32,16,128]{2,1,0:T(8,128)(2,1)S(1)} %shard_map.43), channel_id=1, replica_groups={{0,1,2,3,32,33,34,35,64,65,66,67,96,97,98,99,128,129,130,131,160,161,16..., dimensions={0} | all-to-all | bytes 262144 | tf_op jit(solution)/shard_map/all_to_all | solution.py:269
  47.7 4.4 %shard_map.44 = bf16[32,72,128]{2,1,0:T(8,128)(2,1)S(1)} custom-call(bf16[32,16,128]{2,1,0:T(8,128)(2,1)S(1)} %all_to_all.37.packed_ref, bf16[2,2048,1024]{2,1,0:T(8,128)(2,1)S(1)} %get-tuple-element.9.scans_ref), custom_call_target="tpu_custom_call" | custom-call | tf_op jit(solution)/shard_map/pallas_call | solution.py:216
  52.1 22.6 %all_to_all.38.parts_ref = bf16[32,72,128]{2,1,0:T(8,128)(2,1)S(1)} all-to-all(bf16[32,72,128]{2,1,0:T(8,128)(2,1)S(1)} %shard_map.44), channel_id=1, replica_groups=mesh['subj'=8,'vox'=32] {'vox'}, dimensions={0} | all-to-all | bytes 1179648 | tf_op jit(solution)/shard_map/all_to_all | solution.py:260
  74.8 2.3 %shard_map.45 = f32[8,16,128]{2,1,0:T(8,128)S(1)} custom-call(bf16[32,72,128]{2,1,0:T(8,128)(2,1)S(1)} %all_to_all.38.parts_ref), custom_call_target="tpu_custom_call" | custom-call | tf_op jit(solution)/shard_map/pallas_call | solution.py:216
  77.0 8.0 %all_to_all.39.parts_ref = f32[8,16,128]{2,1,0:T(8,128)S(1)} all-to-all(f32[8,16,128]{2,1,0:T(8,128)S(1)} %shard_map.45), channel_id=1, replica_groups=mesh['subj'=8,'vox'=32] {'subj'}, dimensions={0} | all-to-all | bytes 131072 | tf_op jit(solution)/shard_map/all_to_all | solution.py:263
  85.0 0.2 shard_map.46
  85.1 15.1 %all_to_all.40.packed_ref = bf16[32,16,128]{2,1,0:T(8,128)(2,1)S(1)} all-to-all(bf16[32,16,128]{2,1,0:T(8,128)(2,1)S(1)} %get-tuple-element.11), channel_id=1, replica_groups=mesh['subj'=8,'vox'=32] {'vox'}, dimensions={0} | all-to-all | bytes 262144 | tf_op jit(solution)/shard_map/all_to_all | solution.py:260
  100.3 3.8 %shard_map.47 = (bf16[2,64,2048]{2,1,0:T(8,128)(2,1)S(1)}, bf16[32,40,128]{2,1,0:T(8,128)(2,1)}) custom-call(bf16[32,16,128]{2,1,0:T(8,128)(2,1)S(1)} %all_to_all.40.packed_ref, bf16[2,2048,1024]{2,1,0:T(8,128)(2,1)S(1)} %get-tuple-element.9.scans_ref), custom_call_target="tpu_custom_call" | custom-call | tf_op jit(solution)/shard_map/pallas_call | solution.py:216
  104.0 3.9 %all-to-all-start.6 = ((bf16[32,40,128]{2,1,0:T(8,128)(2,1)}), bf16[32,40,128]{2,1,0:T(8,128)(2,1)S(1)}, u32[]{:S(2)}, u32[]{:S(2)}) async-start(bf16[32,40,128]{2,1,0:T(8,128)(2,1)} %get-tuple-element.12), calls=%async_computation.6 | async-start | bytes 655360 | tf_op jit(solution)/shard_map/all_to_all | solution.py:260
  107.9 0.7 copy.4
  108.6 12.5 %all-to-all-done.6.parts_ref = bf16[32,40,128]{2,1,0:T(8,128)(2,1)S(1)} async-done(((bf16[32,40,128]{2,1,0:T(8,128)(2,1)}), bf16[32,40,128]{2,1,0:T(8,128)(2,1)S(1)}, u32[]{:S(2)}, u32[]{:S(2)}) %all-to-all-start.6) | async-done | bytes 327712 | tf_op jit(solution)/shard_map/all_to_all | solution.py:260
  121.1 3.2 %shard_map.48 = bf16[2,64,2048]{2,1,0:T(8,128)(2,1)} custom-call(bf16[32,40,128]{2,1,0:T(8,128)(2,1)S(1)} %all-to-all-done.6.parts_ref, bf16[2,64,2048]{2,1,0:T(8,128)(2,1)S(1)} %get-tuple-element.13.target_ref), custom_call_target="tpu_custom_call" | custom-call | tf_op jit(solution)/shard_map/pallas_call | solution.py:216
  (2 shorter events, 0.1 us)
Async XLA Ops:
  0.6 1.0 copy-start
  104.0 17.0 %all-to-all-start.6 = ((bf16[32,40,128]{2,1,0:T(8,128)(2,1)}), bf16[32,40,128]{2,1,0:T(8,128)(2,1)S(1)}, u32[]{:S(2)}, u32[]{:S(2)}) async-start(bf16[32,40,128]{2,1,0:T(8,128)(2,1)} %get-tuple-element.12), calls=%async_computation.6 | async-start | bytes 655360 | tf_op jit(solution)/shard_map/all_to_all | solution.py:260

commit v3 on v2

--- a/solution.py
+++ b/solution.py
@@ -15,8 +15,10 @@
 BF16 = jnp.bfloat16
 F32 = jnp.float32
 MIB = 1024 * 1024
-PARAMS = pltpu.CompilerParams(vmem_limit_bytes=24 * MIB)
-START_PARAMS = pltpu.CompilerParams(vmem_limit_bytes=42 * MIB)
+
+
+def vmem(mib):
+    return pltpu.CompilerParams(vmem_limit_bytes=int(mib * MIB))
 
 
 def dot(a, b, contract=(1, 0), precision=None):
@@ -34,20 +36,25 @@
     return high, (x - high.astype(F32)).astype(BF16)
 
 
-def split_dot(a, b):
-    a_high, a_low = halves(a)
-    b_high, b_low = halves(b)
-    left = jnp.concatenate([a_high, a_low], axis=1)
-    right = jnp.concatenate(
-        [
-            jnp.concatenate([b_high, b_low], axis=1),
-            jnp.concatenate([b_high, b_low], axis=1),
-        ],
-        axis=0,
-    )
-    both = dot(left, right)
-    width = b.shape[1]
-    return both[:, :width] + both[:, width:]
+def side_by_side(x):
+    return jnp.concatenate(halves(x), axis=1)
+
+
+def block_diagonal(x):
+    lanes = lax.broadcasted_iota(jnp.int32, x.shape, 1)
+    return jnp.concatenate(
+        [jnp.where(lanes < HALF, x, 0.0), jnp.where(lanes < HALF, 0.0, x)], axis=0
+    )
+
+
+def split_operand(x):
+    wide = side_by_side(block_diagonal(x))
+    return jnp.concatenate([wide, wide], axis=0)
+
+
+def split_dot(left, right):
+    both = dot(side_by_side(left), right)
+    return both[:, :LANES] + both[:, LANES:]
 
 
 def grid_rows_cols(n):
@@ -89,32 +96,27 @@
 
 def polar_factors(first, second):
     rows, cols = grid_rows_cols(HALF)
-    on_diagonal = rows == cols
-    zero = jnp.zeros((HALF, HALF), F32)
 
     def trace(gram):
-        return jnp.sum(jnp.where(on_diagonal, gram, 0.0), keepdims=True)
-
-    squares = trace(first), trace(second)
-    gram = jnp.concatenate(
-        [
-            jnp.concatenate([first / squares[0], zero], axis=1),
-            jnp.concatenate([zero, second / squares[1]], axis=1),
-        ],
-        axis=0,
-    )
-    big_rows, big_cols = grid_rows_cols(LANES)
-    identity = jnp.where(big_rows == big_cols, 1.0, 0.0)
-    factor = None
-    for step in range(ITERS):
+        return jnp.sum(jnp.where(rows == cols, gram, 0.0), keepdims=True)
+
+    wide_rows = lax.broadcasted_iota(jnp.int32, (HALF, LANES), 0)
+    lanes = lax.broadcasted_iota(jnp.int32, (HALF, LANES), 1)
+    identity = jnp.where(wide_rows == lanes % HALF, 1.0, 0.0)
+    squares = jnp.where(lanes[:1] < HALF, trace(first), trace(second))
+    gram = jnp.concatenate([first, second], axis=1) / squares
+    factor = polar = 1.5 * identity - 0.5 * gram
+    for step in range(1, ITERS):
+        half_way = split_dot(polar, split_operand(gram))
+        right = split_operand(polar)
+        if step == 1:
+            gram = split_dot(half_way, right)
+        else:
+            both = split_dot(jnp.concatenate([half_way, factor], axis=0), right)
+            gram, factor = both[:HALF], both[HALF:]
         polar = 1.5 * identity - 0.5 * gram
-        factor = polar if factor is None else split_dot(polar, factor)
-        if step < ITERS - 1:
-            gram = split_dot(split_dot(polar, gram), polar)
-    scale = jnp.where(
-        big_rows[:, :1] < HALF, lax.rsqrt(squares[0]), lax.rsqrt(squares[1])
-    )
-    return factor * scale
+    factor = split_dot(factor, split_operand(polar))
+    return factor * lax.rsqrt(squares)
 
 
 def start_kernel(tile, maps_ref, scans_ref, out_ref, held, maps, maps_sem, sems):
@@ -151,57 +153,66 @@
 def spread_last_kernel(parts_ref, out_ref, resp_ref):
     summed = jnp.sum(parts_ref[...], axis=0)
     out_ref[...] = jnp.broadcast_to(summed.astype(BF16)[None], out_ref.shape)
-    resp_ref[...] = unpack_frames(summed[None]).T
+    resp_ref[...] = summed
+
+
+def targets_of(packed_ref, scans_ref):
+    shared = unpack_frames(packed_ref[...]).T
+    target = jnp.concatenate(
+        [dot(shared, scans_ref[subject], (1, 1)).astype(BF16) for subject in range(2)],
+        axis=0,
+    )
+    gram = dot(target, target, (1, 1))
+    return target, pack_grams(gram[:HALF, :HALF], gram[HALF:, HALF:])
 
 
 def middle_kernel(packed_ref, scans_ref, out_ref):
-    shared = unpack_frames(packed_ref[...]).T
-    grams, onward = [], []
-    for subject in range(2):
-        scans = scans_ref[subject]
-        target = dot(shared, scans, (1, 1)).astype(BF16)
-        grams.append(dot(target, target, (1, 1)))
-        onward.append(dot(target, scans).T)
+    target, packed = targets_of(packed_ref, scans_ref)
+    onward = [dot(target[:HALF], scans_ref[0]), dot(target[HALF:], scans_ref[1])]
     shares = out_ref.shape[0]
-    by_frame = jnp.concatenate(onward, axis=1).reshape(shares, 32, LANES)
-    packed = pack_grams(*grams)
+    by_frame = jnp.concatenate(onward, axis=0).T.reshape(shares, 32, LANES)
     packed = jnp.broadcast_to(packed[None], (shares,) + packed.shape)
     out_ref[...] = jnp.concatenate([by_frame, packed], axis=1).astype(BF16)
 
 
 def polar_share_kernel(scale, parts_ref, out_ref):
     summed = jnp.sum(parts_ref[...].astype(F32), axis=0)
-    factor = polar_factors(*unpack_grams(summed[32:]))
-    stacked = jnp.concatenate([factor[:HALF, :HALF], factor[HALF:, HALF:]], axis=0)
-    high, low = halves(summed[:32])
-    stack_high, stack_low = halves(stacked)
-    share = dot(high, stack_high) + dot(low, stack_high) + dot(high, stack_low)
-    share *= scale
-    packed = pack_frames(share)
-    out_ref[...] = jnp.broadcast_to(packed, out_ref.shape)
+    factor = polar_factors(*unpack_grams(summed[32:])) * scale
+    share = split_dot(summed[:32], split_operand(factor))
+    share = share[:, :HALF] + share[:, HALF:]
+    out_ref[...] = jnp.broadcast_to(pack_frames(share), out_ref.shape)
 
 
 def target_kernel(packed_ref, scans_ref, target_ref, out_ref):
-    shared = unpack_frames(packed_ref[...]).T
-    grams = []
-    for subject in range(2):
-        target = dot(shared, scans_ref[subject], (1, 1)).astype(BF16)
-        target_ref[subject] = target
-        grams.append(dot(target, target, (1, 1)))
-    packed = pack_grams(*grams).astype(BF16)
-    out_ref[...] = jnp.broadcast_to(packed[None], out_ref.shape)
-
-
-def maps_kernel(scale, parts_ref, target_ref, out_ref):
+    target, packed = targets_of(packed_ref, scans_ref)
+    target_ref[...] = target
+    out_ref[...] = jnp.broadcast_to(packed.astype(BF16)[None], out_ref.shape)
+
+
+def maps_kernel(
+    scale, pieces, parts_ref, target_ref, share_ref, out_ref, resp_ref, maps, resp, sems
+):
+    resp[...] = unpack_frames(share_ref[...][None])
+    copies = [pltpu.make_async_copy(resp, resp_ref, sems.at[pieces])]
+    copies[0].start()
     summed = jnp.sum(parts_ref[...].astype(F32), axis=0)
     factor = polar_factors(*unpack_grams(summed)) * scale
-    high = factor.astype(BF16)
-    low = (factor - high.astype(F32)).astype(BF16)
-    for subject in range(2):
-        own = slice(subject * HALF, (subject + 1) * HALF)
-        target = target_ref[subject]
-        maps = dot(high[own, own], target) + dot(low[own, own], target)
-        out_ref[subject] = maps.astype(BF16)
+    left = side_by_side(block_diagonal(factor))
+    target = target_ref[...]
+    width = target.shape[1] // pieces
+    for piece in range(pieces):
+        part = slice(piece * width, (piece + 1) * width)
+        right = jnp.concatenate([target[:, part], target[:, part]], axis=0)
+        made = dot(left, right).astype(BF16)
+        maps[:, :, part] = made.reshape(maps.shape[:2] + (width,))
+        copies.append(
+            pltpu.make_async_copy(
+                maps.at[:, :, part], out_ref.at[:, :, part], sems.at[piece]
+            )
+        )
+        copies[-1].start()
+    for copy in copies:
+        copy.wait()
 
 
 VMEM = pl.BlockSpec(memory_space=pltpu.VMEM)
@@ -212,14 +223,24 @@
     return jax.ShapeDtypeStruct(shape, dtype)
 
 
-def small(body, out_shape, *args):
+def call(body, mib, out_shape, args, arg_specs, out_specs, scratch=()):
     return pl.pallas_call(
         body,
         out_shape=out_shape,
-        in_specs=[VMEM] * len(args),
-        out_specs=jax.tree.map(lambda _: VMEM, out_shape),
-        compiler_params=PARAMS,
+        in_specs=arg_specs,
+        out_specs=out_specs,
+        scratch_shapes=scratch,
+        compiler_params=vmem(mib),
     )(*args)
+
+
+def small(body, out_shape, *args):
+    out_specs = jax.tree.map(lambda _: VMEM, out_shape)
+    return call(body, 24, out_shape, args, [VMEM] * len(args), out_specs)
+
+
+def copies_of(count):
+    return pltpu.SemaphoreType.DMA((count,))
 
 
 def start(maps, scans, shares, tile):
@@ -235,9 +256,9 @@
         scratch_shapes=[
             pltpu.VMEM(maps.shape, maps.dtype),
             pltpu.SemaphoreType.DMA,
-            pltpu.SemaphoreType.DMA((subj_dev * (vox_dev // tile),)),
+            copies_of(subj_dev * (vox_dev // tile)),
         ],
-        compiler_params=START_PARAMS,
+        compiler_params=vmem(42),
     )(maps, scans)
 
 
@@ -276,36 +297,39 @@
     shared = small(spread_kernel, shape_of((shares,) + share, BF16), parts)
     shared = across_subj_x(shared)
 
-    partial = small(
-        middle_kernel, shape_of((vox_ways, 72, LANES), BF16), shared, scans
-    )
-    parts = across_vox(partial)
+    gathered = shape_of((vox_ways, 72, LANES), BF16)
+    parts = across_vox(small(middle_kernel, gathered, shared, scans))
     share_sum = functools.partial(polar_share_kernel, 1.0 / subjects)
     parts = across_subj(small(share_sum, shape_of((subj_ways,) + share, F32), parts))
-    shared, shared_resp = small(
+    shared, own_share = small(
         spread_last_kernel,
-        [shape_of((vox_ways,) + share, BF16), shape_of((features, 32), F32)],
+        [shape_of((vox_ways,) + share, BF16), shape_of(share, F32)],
         parts,
     )
     shared = across_vox(shared)
 
-    target, partial = small(
-        target_kernel,
+    target_shapes = [
+        shape_of((subj_dev * features, vox_dev), BF16),
+        shape_of((vox_ways, 40, LANES), BF16),
+    ]
+    target, partial = small(target_kernel, target_shapes, shared, scans)
+    parts = across_vox(partial)
+    maps_shape = (subj_dev, features, vox_dev)
+    pieces = 4
+    subject_maps, shared_resp = call(
+        functools.partial(maps_kernel, math.sqrt(voxels), pieces),
+        20,
+        [shape_of(maps_shape, BF16), shape_of((32, features), F32)],
+        (parts, target, own_share),
+        [VMEM] * 3,
+        [HBM] * 2,
         [
-            shape_of((subj_dev, features, vox_dev), BF16),
-            shape_of((vox_ways, 40, LANES), BF16),
+            pltpu.VMEM(maps_shape, BF16),
+            pltpu.VMEM((32, features), F32),
+            copies_of(pieces + 1),
         ],
-        shared,
-        scans,
-    )
-    parts = across_vox(partial)
-    subject_maps = small(
-        functools.partial(maps_kernel, math.sqrt(voxels)),
-        shape_of((subj_dev, features, vox_dev), BF16),
-        parts,
-        target,
-    )
-    return (shared_resp, subject_maps)
+    )
+    return (shared_resp.T, subject_maps)
 
 
 def solution(mesh):

time: 125 us -> 123 us (0.984)
  blocking collectives: 87.6 us -> 104 us
  waiting for transfers between devices: 12.5 us -> 0 us
  starting transfers between devices: 3.88 us -> 0 us
  Pallas kernels: 17.9 us -> 16.6 us
    all_to_all x2 -> x3, blocking collectives: 37.8 us -> 54.3 us  [across_vox(): return lax.all_to_all(x, 'vox', 0, 0)]
    all_to_all x1 -> x0, waiting for transfers between devices: 12.5 us -> none  [across_vox(): return lax.all_to_all(x, 'vox', 0, 0)]
    all_to_all x1 -> x0, starting transfers between devices: 3.88 us -> none  [across_vox(): return lax.all_to_all(x, 'vox', 0, 0)]
    pallas_call x7, Pallas kernels: 13.8 us -> 12.5 us  [call(): pl.pallas_call(body, out_shape=out_shape, in_specs=arg_specs, out_specs=o...]
  transfers between devices with their start and end apart: 1 -> 0, of which waited for: 1 -> 0; matrix products, arithmetic and copies ran while one was open for 1% -> 0% of each run, Pallas kernels for 0% -> 0%
where the time goes in v3:
time: 123 us; the launch traced here: 122 us
  blocking collectives  104 us (85%)
  Pallas kernels  16.6 us (13%)
    all_to_all x3, blocking collectives, across_vox(): return lax.all_to_all(x, 'vox', 0, 0)  54.3 us
    all_to_all x2, blocking collectives, across_subj_x(): return lax.all_to_all(x, ('subj', 'vox'), 0, 0, axis_index_groups=same_z)  25.3 us
    all_to_all x1, blocking collectives, across_z(): return lax.all_to_all(x, 'vox', 0, 0, axis_index_groups=same_x)  16.6 us
    pallas_call x7, Pallas kernels, call(): pl.pallas_call(body, out_shape=out_shape, in_specs=arg_specs, out_specs=o...  12.5 us
    all_to_all x1, blocking collectives, across_subj(): return lax.all_to_all(x, 'subj', 0, 0)  7.96 us
    pallas_call x1, Pallas kernels, start(): pl.pallas_call(functools.partial(start_kernel, tile), out_shape=[shape_of...  4.03 us

profile of v3, /device:TPU:8, one launch (start us, length us, event | category | flops | bytes accessed | tf_op | source)
XLA Modules:
  0.0 122.5 jit_solution(8535983761561674124)
XLA Ops:
  0.6 0.0 copy-start
  0.6 1.0 copy-done
  1.7 4.0 %shard_map.41 = (bf16[32,16,128]{2,1,0:T(8,128)(2,1)S(1)}, bf16[2,2048,1024]{2,1,0:T(8,128)(2,1)S(1)}) custom-call(bf16[2,64,2048]{2,1,0:T(8,128)(2,1)S(1)} %copy-done, bf16[2,2048,1024]{2,1,0:T(8,128)(2,1)} %scans_ref.1), custom_call_target="tpu_custom_call" | custom-call | tf_op jit(solution)/shard_map/pallas_call | solution.py:248
  5.7 13.8 %all_to_all.35.parts_ref = bf16[32,16,128]{2,1,0:T(8,128)(2,1)S(1)} all-to-all(bf16[32,16,128]{2,1,0:T(8,128)(2,1)S(1)} %get-tuple-element.10), channel_id=1, replica_groups={{0,1,2,3,32,33,34,35,64,65,66,67,96,97,98,99,128,129,130,131,160,161,16..., dimensions={0} | all-to-all | bytes 262144 | tf_op jit(solution)/shard_map/all_to_all | solution.py:290
  19.6 16.6 %all_to_all.36.parts_ref = f32[8,16,128]{2,1,0:T(8,128)S(1)} all-to-all(f32[8,16,128]{2,1,0:T(8,128)S(1)} %shard_map.42), channel_id=1, replica_groups={{0,4,8,12,16,20,24,28},{1,5,9,13,17,21,25,29},{2,6,10,14,18,22,26,30},{..., dimensions={0} | all-to-all | bytes 131072 | tf_op jit(solution)/shard_map/all_to_all | solution.py:287
  36.3 11.5 %all_to_all.37.packed_ref = bf16[32,16,128]{2,1,0:T(8,128)(2,1)S(1)} all-to-all(bf16[32,16,128]{2,1,0:T(8,128)(2,1)S(1)} %shard_map.43), channel_id=1, replica_groups={{0,1,2,3,32,33,34,35,64,65,66,67,96,97,98,99,128,129,130,131,160,161,16..., dimensions={0} | all-to-all | bytes 262144 | tf_op jit(solution)/shard_map/all_to_all | solution.py:290
  47.7 4.3 %shard_map.44 = bf16[32,72,128]{2,1,0:T(8,128)(2,1)S(1)} custom-call(bf16[32,16,128]{2,1,0:T(8,128)(2,1)S(1)} %all_to_all.37.packed_ref, bf16[2,2048,1024]{2,1,0:T(8,128)(2,1)S(1)} %get-tuple-element.11.scans_ref), custom_call_target="tpu_custom_call" | custom-call | tf_op jit(solution)/shard_map/pallas_call | solution.py:227
  52.1 22.6 %all_to_all.38.parts_ref = bf16[32,72,128]{2,1,0:T(8,128)(2,1)S(1)} all-to-all(bf16[32,72,128]{2,1,0:T(8,128)(2,1)S(1)} %shard_map.44), channel_id=1, replica_groups=mesh['subj'=8,'vox'=32] {'vox'}, dimensions={0} | all-to-all | bytes 1179648 | tf_op jit(solution)/shard_map/all_to_all | solution.py:281
  74.7 2.2 %shard_map.45 = f32[8,16,128]{2,1,0:T(8,128)S(1)} custom-call(bf16[32,72,128]{2,1,0:T(8,128)(2,1)S(1)} %all_to_all.38.parts_ref), custom_call_target="tpu_custom_call" | custom-call | tf_op jit(solution)/shard_map/pallas_call | solution.py:227
  76.9 8.0 %all_to_all.39.parts_ref = f32[8,16,128]{2,1,0:T(8,128)S(1)} all-to-all(f32[8,16,128]{2,1,0:T(8,128)S(1)} %shard_map.45), channel_id=1, replica_groups=mesh['subj'=8,'vox'=32] {'subj'}, dimensions={0} | all-to-all | bytes 131072 | tf_op jit(solution)/shard_map/all_to_all | solution.py:284
  84.9 15.2 %all_to_all.40.packed_ref = bf16[32,16,128]{2,1,0:T(8,128)(2,1)S(1)} all-to-all(bf16[32,16,128]{2,1,0:T(8,128)(2,1)S(1)} %get-tuple-element.12), channel_id=1, replica_groups=mesh['subj'=8,'vox'=32] {'vox'}, dimensions={0} | all-to-all | bytes 262144 | tf_op jit(solution)/shard_map/all_to_all | solution.py:281
  100.0 3.0 %shard_map.47 = (bf16[128,2048]{1,0:T(8,128)(2,1)S(1)}, bf16[32,40,128]{2,1,0:T(8,128)(2,1)S(1)}) custom-call(bf16[32,16,128]{2,1,0:T(8,128)(2,1)S(1)} %all_to_all.40.packed_ref, bf16[2,2048,1024]{2,1,0:T(8,128)(2,1)S(1)} %get-tuple-element.11.scans_ref), custom_call_target="tpu_custom_call" | custom-call | tf_op jit(solution)/shard_map/pallas_call | solution.py:227
  103.0 16.5 %all_to_all.41.parts_ref = bf16[32,40,128]{2,1,0:T(8,128)(2,1)S(1)} all-to-all(bf16[32,40,128]{2,1,0:T(8,128)(2,1)S(1)} %get-tuple-element.13), channel_id=1, replica_groups=mesh['subj'=8,'vox'=32] {'vox'}, dimensions={0} | all-to-all | bytes 655360 | tf_op jit(solution)/shard_map/all_to_all | solution.py:281
  119.6 2.9 %shard_map.48 = (bf16[2,64,2048]{2,1,0:T(8,128)(2,1)}, f32[32,64]{1,0:T(8,128)}) custom-call(bf16[32,40,128]{2,1,0:T(8,128)(2,1)S(1)} %all_to_all.41.parts_ref, bf16[128,2048]{1,0:T(8,128)(2,1)S(1)} %get-tuple-element.14.target_ref, f32[16,128]{1,0:T(8,128)S(1)} %get-tuple-element.15.share_ref), custom_call_target="tpu_custom_call" | custom-call | tf_op jit(solution)/shard_map/pallas_call | solution.py:227
  (3 shorter events, 0.1 us)
Async XLA Ops:
  0.6 1.0 copy-start

commit v4 on v3

--- a/solution.py
+++ b/solution.py
@@ -142,16 +142,16 @@
 
 def add_kernel(scale, parts_ref, out_ref):
     summed = jnp.sum(parts_ref[...].astype(F32), axis=0) * scale
-    out_ref[...] = jnp.broadcast_to(summed[None], out_ref.shape)
+    out_ref[...] = jnp.broadcast_to(summed.astype(BF16)[None], out_ref.shape)
 
 
 def spread_kernel(parts_ref, out_ref):
-    summed = jnp.sum(parts_ref[...], axis=0)
+    summed = jnp.sum(parts_ref[...].astype(F32), axis=0)
     out_ref[...] = jnp.broadcast_to(summed.astype(BF16)[None], out_ref.shape)
 
 
 def spread_last_kernel(parts_ref, out_ref, resp_ref):
-    summed = jnp.sum(parts_ref[...], axis=0)
+    summed = jnp.sum(parts_ref[...].astype(F32), axis=0)
     out_ref[...] = jnp.broadcast_to(summed.astype(BF16)[None], out_ref.shape)
     resp_ref[...] = summed
 
@@ -169,10 +169,21 @@
 def middle_kernel(packed_ref, scans_ref, out_ref):
     target, packed = targets_of(packed_ref, scans_ref)
     onward = [dot(target[:HALF], scans_ref[0]), dot(target[HALF:], scans_ref[1])]
-    shares = out_ref.shape[0]
-    by_frame = jnp.concatenate(onward, axis=0).T.reshape(shares, 32, LANES)
-    packed = jnp.broadcast_to(packed[None], (shares,) + packed.shape)
-    out_ref[...] = jnp.concatenate([by_frame, packed], axis=1).astype(BF16)
+    by_frame = jnp.concatenate(onward, axis=0).T.astype(BF16)
+    packed = packed.astype(BF16)
+    ways = out_ref.shape[0]
+    shares = by_frame.shape[0] // 32
+    for x in range(ways):
+        own = [by_frame[v * 32 : (v + 1) * 32] for v in range(x, shares, ways)]
+        out_ref[x] = jnp.concatenate(own + [packed], axis=0)
+
+
+def regroup_kernel(parts_ref, out_ref):
+    summed = jnp.sum(parts_ref[...].astype(F32), axis=0).astype(BF16)
+    ways = out_ref.shape[0]
+    packed = summed[ways * 32 :]
+    for z in range(ways):
+        out_ref[z] = jnp.concatenate([summed[z * 32 : (z + 1) * 32], packed], axis=0)
 
 
 def polar_share_kernel(scale, parts_ref, out_ref):
@@ -180,7 +191,8 @@
     factor = polar_factors(*unpack_grams(summed[32:])) * scale
     share = split_dot(summed[:32], split_operand(factor))
     share = share[:, :HALF] + share[:, HALF:]
-    out_ref[...] = jnp.broadcast_to(pack_frames(share), out_ref.shape)
+    packed = pack_frames(share).astype(BF16)
+    out_ref[...] = jnp.broadcast_to(packed, out_ref.shape)
 
 
 def target_kernel(packed_ref, scans_ref, target_ref, out_ref):
@@ -272,6 +284,7 @@
     share = (16, LANES)
     z_ways = vox_ways // X_WAYS
     same_x = [[z * X_WAYS + x for z in range(z_ways)] for x in range(X_WAYS)]
+    own_z = [[z * X_WAYS + x for x in range(X_WAYS)] for z in range(z_ways)]
     same_z = [
         [s * vox_ways + z * X_WAYS + x for s in range(subj_ways) for x in range(X_WAYS)]
         for z in range(z_ways)
@@ -286,6 +299,9 @@
     def across_z(x):
         return lax.all_to_all(x, "vox", 0, 0, axis_index_groups=same_x)
 
+    def across_x(x):
+        return lax.all_to_all(x, "vox", 0, 0, axis_index_groups=own_z)
+
     def across_subj_x(x):
         return lax.all_to_all(x, ("subj", "vox"), 0, 0, axis_index_groups=same_z)
 
@@ -293,14 +309,16 @@
     partial, scans = start(start_maps, scans, shares, 512)
     parts = across_subj_x(partial)
     summed = functools.partial(add_kernel, norm_scale)
-    parts = across_z(small(summed, shape_of((z_ways,) + share, F32), parts))
+    parts = across_z(small(summed, shape_of((z_ways,) + share, BF16), parts))
     shared = small(spread_kernel, shape_of((shares,) + share, BF16), parts)
     shared = across_subj_x(shared)
 
-    gathered = shape_of((vox_ways, 72, LANES), BF16)
-    parts = across_vox(small(middle_kernel, gathered, shared, scans))
+    by_x = shape_of((X_WAYS, z_ways * 32 + 40, LANES), BF16)
+    parts = across_x(small(middle_kernel, by_x, shared, scans))
+    by_z = shape_of((z_ways, 72, LANES), BF16)
+    parts = across_z(small(regroup_kernel, by_z, parts))
     share_sum = functools.partial(polar_share_kernel, 1.0 / subjects)
-    parts = across_subj(small(share_sum, shape_of((subj_ways,) + share, F32), parts))
+    parts = across_subj(small(share_sum, shape_of((subj_ways,) + share, BF16), parts))
     shared, own_share = small(
         spread_last_kernel,
         [shape_of((vox_ways,) + share, BF16), shape_of(share, F32)],

time: 123 us -> 120 us (0.976)
  blocking collectives: 104 us -> 101 us
    all_to_all x3 -> x2, blocking collectives: 54.3 us -> 30.3 us  [across_vox(): return lax.all_to_all(x, 'vox', 0, 0)]
    all_to_all x1 -> x2, blocking collectives: 16.6 us -> 27.9 us  [across_z(): return lax.all_to_all(x, 'vox', 0, 0, axis_index_groups=same_x)]
    all_to_all x0 -> x1, blocking collectives: none -> 10.1 us  [across_x(): return lax.all_to_all(x, 'vox', 0, 0, axis_index_groups=own_z)]
    pallas_call x7 -> x8, Pallas kernels: 12.5 us -> 12.5 us  [call(): pl.pallas_call(body, out_shape=out_shape, in_specs=arg_specs, out_specs=o...]
where the time goes in v4:
time: 120 us
  blocking collectives  101 us (84%)
  Pallas kernels  16.6 us (14%)
    all_to_all x2, blocking collectives, across_vox(): return lax.all_to_all(x, 'vox', 0, 0)  30.3 us
    all_to_all x2, blocking collectives, across_z(): return lax.all_to_all(x, 'vox', 0, 0, axis_index_groups=same_x)  27.9 us
    all_to_all x2, blocking collectives, across_subj_x(): return lax.all_to_all(x, ('subj', 'vox'), 0, 0, axis_index_groups=same_z)  25.3 us
    pallas_call x8, Pallas kernels, call(): pl.pallas_call(body, out_shape=out_shape, in_specs=arg_specs, out_specs=o...  12.5 us
    all_to_all x1, blocking collectives, across_x(): return lax.all_to_all(x, 'vox', 0, 0, axis_index_groups=own_z)  10.1 us
    all_to_all x1, blocking collectives, across_subj(): return lax.all_to_all(x, 'subj', 0, 0)  7.79 us
    pallas_call x1, Pallas kernels, start(): pl.pallas_call(functools.partial(start_kernel, tile), out_shape=[shape_of...  4.03 us

profile of v4, /device:TPU:8, one launch (start us, length us, event | category | flops | bytes accessed | tf_op | source)
XLA Modules:
  0.0 119.8 jit_solution(14278022783756191903)
XLA Ops:
  0.6 0.0 copy-start
  0.6 1.0 copy-done
  1.7 4.0 %shard_map.41 = (bf16[32,16,128]{2,1,0:T(8,128)(2,1)S(1)}, bf16[2,2048,1024]{2,1,0:T(8,128)(2,1)S(1)}) custom-call(bf16[2,64,2048]{2,1,0:T(8,128)(2,1)S(1)} %copy-done, bf16[2,2048,1024]{2,1,0:T(8,128)(2,1)} %scans_ref.1), custom_call_target="tpu_custom_call" | custom-call | tf_op jit(solution)/shard_map/pallas_call | solution.py:260
  5.7 13.8 %all_to_all.40.parts_ref = bf16[32,16,128]{2,1,0:T(8,128)(2,1)S(1)} all-to-all(bf16[32,16,128]{2,1,0:T(8,128)(2,1)S(1)} %get-tuple-element.10), channel_id=1, replica_groups={{0,1,2,3,32,33,34,35,64,65,66,67,96,97,98,99,128,129,130,131,160,161,16..., dimensions={0} | all-to-all | bytes 262144 | tf_op jit(solution)/shard_map/all_to_all | solution.py:306
  19.6 16.3 %all_to_all.41.parts_ref = bf16[8,16,128]{2,1,0:T(8,128)(2,1)S(1)} all-to-all(bf16[8,16,128]{2,1,0:T(8,128)(2,1)S(1)} %shard_map.42), channel_id=1, replica_groups={{0,4,8,12,16,20,24,28},{1,5,9,13,17,21,25,29},{2,6,10,14,18,22,26,30},{..., dimensions={0} | all-to-all | bytes 65536 | tf_op jit(solution)/shard_map/all_to_all | solution.py:300
  35.9 11.5 %all_to_all.42.packed_ref = bf16[32,16,128]{2,1,0:T(8,128)(2,1)S(1)} all-to-all(bf16[32,16,128]{2,1,0:T(8,128)(2,1)S(1)} %shard_map.43), channel_id=1, replica_groups={{0,1,2,3,32,33,34,35,64,65,66,67,96,97,98,99,128,129,130,131,160,161,16..., dimensions={0} | all-to-all | bytes 262144 | tf_op jit(solution)/shard_map/all_to_all | solution.py:306
  47.4 4.4 %shard_map.44 = bf16[4,296,128]{2,1,0:T(8,128)(2,1)S(1)} custom-call(bf16[32,16,128]{2,1,0:T(8,128)(2,1)S(1)} %all_to_all.42.packed_ref, bf16[2,2048,1024]{2,1,0:T(8,128)(2,1)S(1)} %get-tuple-element.11.scans_ref), custom_call_target="tpu_custom_call" | custom-call | tf_op jit(solution)/shard_map/pallas_call | solution.py:239
  51.7 10.1 %all_to_all.43.parts_ref = bf16[4,296,128]{2,1,0:T(8,128)(2,1)S(1)} all-to-all(bf16[4,296,128]{2,1,0:T(8,128)(2,1)S(1)} %shard_map.44), channel_id=1, replica_groups={{0,1,2,3},{4,5,6,7},{8,9,10,11},{12,13,14,15},{16,17,18,19},{20,21,22,2..., dimensions={0} | all-to-all | bytes 606208 | tf_op jit(solution)/shard_map/all_to_all | solution.py:303
  61.9 11.6 %all_to_all.44.parts_ref = bf16[8,72,128]{2,1,0:T(8,128)(2,1)S(1)} all-to-all(bf16[8,72,128]{2,1,0:T(8,128)(2,1)S(1)} %shard_map.45), channel_id=1, replica_groups={{0,4,8,12,16,20,24,28},{1,5,9,13,17,21,25,29},{2,6,10,14,18,22,26,30},{..., dimensions={0} | all-to-all | bytes 294912 | tf_op jit(solution)/shard_map/all_to_all | solution.py:300
  73.5 2.1 %shard_map.46 = bf16[8,16,128]{2,1,0:T(8,128)(2,1)S(1)} custom-call(bf16[8,72,128]{2,1,0:T(8,128)(2,1)S(1)} %all_to_all.44.parts_ref), custom_call_target="tpu_custom_call" | custom-call | tf_op jit(solution)/shard_map/pallas_call | solution.py:239
  75.7 7.8 %all_to_all.45.parts_ref = bf16[8,16,128]{2,1,0:T(8,128)(2,1)S(1)} all-to-all(bf16[8,16,128]{2,1,0:T(8,128)(2,1)S(1)} %shard_map.46), channel_id=1, replica_groups=mesh['subj'=8,'vox'=32] {'subj'}, dimensions={0} | all-to-all | bytes 65536 | tf_op jit(solution)/shard_map/all_to_all | solution.py:297
  83.5 13.7 %all_to_all.46.packed_ref = bf16[32,16,128]{2,1,0:T(8,128)(2,1)S(1)} all-to-all(bf16[32,16,128]{2,1,0:T(8,128)(2,1)S(1)} %get-tuple-element.12), channel_id=1, replica_groups=mesh['subj'=8,'vox'=32] {'vox'}, dimensions={0} | all-to-all | bytes 262144 | tf_op jit(solution)/shard_map/all_to_all | solution.py:294
  97.2 3.0 %shard_map.48 = (bf16[128,2048]{1,0:T(8,128)(2,1)S(1)}, bf16[32,40,128]{2,1,0:T(8,128)(2,1)S(1)}) custom-call(bf16[32,16,128]{2,1,0:T(8,128)(2,1)S(1)} %all_to_all.46.packed_ref, bf16[2,2048,1024]{2,1,0:T(8,128)(2,1)S(1)} %get-tuple-element.11.scans_ref), custom_call_target="tpu_custom_call" | custom-call | tf_op jit(solution)/shard_map/pallas_call | solution.py:239
  100.3 16.6 %all_to_all.47.parts_ref = bf16[32,40,128]{2,1,0:T(8,128)(2,1)S(1)} all-to-all(bf16[32,40,128]{2,1,0:T(8,128)(2,1)S(1)} %get-tuple-element.13), channel_id=1, replica_groups=mesh['subj'=8,'vox'=32] {'vox'}, dimensions={0} | all-to-all | bytes 655360 | tf_op jit(solution)/shard_map/all_to_all | solution.py:294
  116.9 2.9 %shard_map.49 = (bf16[2,64,2048]{2,1,0:T(8,128)(2,1)}, f32[32,64]{1,0:T(8,128)}) custom-call(bf16[32,40,128]{2,1,0:T(8,128)(2,1)S(1)} %all_to_all.47.parts_ref, bf16[128,2048]{1,0:T(8,128)(2,1)S(1)} %get-tuple-element.14.target_ref, f32[16,128]{1,0:T(8,128)S(1)} %get-tuple-element.15.share_ref), custom_call_target="tpu_custom_call" | custom-call | tf_op jit(solution)/shard_map/pallas_call | solution.py:239
  (4 shorter events, 0.1 us)
Async XLA Ops:
  0.6 1.0 copy-start
